TPU v7x, 32 devices: a whole 2x2x4 slice. The times are simulated.
32 devices in a mesh: dp: 8 (over z, core), ctx: 4 (over y, x).
Axes of the slice: x: 2, y: 2, z: 4, core: 2. Of those that a mesh axis runs over, the one named last changes fastest.
Arguments:
- gene_ids: int32 [8, 512], P('dp', 'ctx'), may hold values from 0 to 9631, as said below
- counts: int32 [8, 512], P('dp', 'ctx'), may hold values from 1 to 1024
- values: float32 [8, 512], P('dp', 'ctx'), may hold values from -6 to 6
- lengths: int32 [8], P('dp'), may hold values from 1 to 512, 1365 in all
- bin_edges: int32 [8, 50], P('dp'), may hold values from 1 to 1024, as said below
- bin_table: bfloat16 [51, 384], replicated, may hold values from -6 to 6
- value_weight: float32 [384], replicated, may hold values from -6 to 6
- in_weight: bfloat16 [384, 2048], P(None, 'dp'), may hold values from -0.3125 to 0.3125
- out_weight: bfloat16 [2048, 384], P('dp'), may hold values from -0.125 to 0.125
- gene_table: bfloat16 [9632, 384], P('ctx'), may hold values from -6 to 6
- zero_embed: bfloat16 [384], replicated, may hold values from -6 to 6
- qkv_weight: bfloat16 [384, 1152], replicated, may hold values from -0.3125 to 0.3125
- proj_weight: bfloat16 [384, 384], replicated, may hold values from -0.3125 to 0.3125
- readout: float32 [384], replicated, may hold values from -0.3125 to 0.3125
- targets: float32 [8, 9632], P('dp', 'ctx'), may hold values from -6 to 6
Outputs:
- predicted: float32 [8, 9632], P('dp', 'ctx')
- grad_qkv: float32 [384, 1152], P('dp', 'ctx')
Inputs may be any that keep to these rules, and one draw needn't show every extreme that they name: `gene_ids`: within one cell all entries are distinct. Of the 128 entries of one cell held by one index of ctx, exactly 32 lie in each block of 2408 consecutive genes. Entries at positions from the cell's length on are unused. `bin_edges`: strictly increasing along each row; the last edge of every cell is 1024. `lengths`: they sum to 1365 and the largest is 512.
All inputs are finite; a program needn't handle non-finite values. No bound on the sum of `lengths` on one device may be relied on, other than what follows from the above.
Results may differ from a plain program's by a relative error of at most 0.003.
The roundings to bfloat16 on the way count: a program that leaves them out, or rounds other values in their place, can miss the bound.
Values may be sent and summed in bfloat16 or wider, within the bound.
A program may use at most 128 MiB of HBM per device.

v0:
```python
import math

import jax
import jax.numpy as jnp
from jax import lax
from jax.sharding import PartitionSpec as P

HEAD = 64
HEADS = 6


feature_scale = 2.5
norm_eps = 1e-06
highest = lax.Precision.HIGHEST


def featurize(projected):
    inverse = lax.rsqrt(jnp.mean(projected * projected, axis=-1, keepdims=True) + norm_eps)
    return jnp.exp(feature_scale * projected * inverse)


def rms_round(matrix):
    inverse = lax.rsqrt(jnp.mean(matrix * matrix, axis=-1, keepdims=True) + norm_eps)
    return (matrix * inverse).astype(jnp.bfloat16)


def embed_tokens(token_counts, token_values, cell_edges, bin_table, value_weight):
    binned = jnp.sum((token_counts[:, None] >= cell_edges[None, :]).astype(jnp.int32), axis=1)
    one_hot = (binned[:, None] == jnp.arange(bin_table.shape[0], dtype=jnp.int32)[None, :]).astype(
        jnp.bfloat16
    )
    looked = jnp.dot(one_hot, bin_table, preferred_element_type=jnp.float32)
    return looked + token_values[:, None] * value_weight[None, :]


def encode(token_counts, token_values, cell_edges, bin_table, value_weight, in_weight, out_weight):
    embedded = embed_tokens(token_counts, token_values, cell_edges, bin_table, value_weight)
    normed_tokens = rms_round(embedded)
    activated = jax.nn.silu(
        jnp.dot(
            normed_tokens,
            lax.all_gather(in_weight, "dp", axis=1, tiled=True),
            preferred_element_type=jnp.float32,
        )
    ).astype(jnp.bfloat16)
    mixed = embedded + jnp.dot(
        activated,
        lax.all_gather(out_weight, "dp", axis=0, tiled=True),
        preferred_element_type=jnp.float32,
    )
    return mixed.astype(jnp.bfloat16)


def assemble(gene_rows, local_index, arrived, zero_embed):
    row_count = gene_rows.shape[0]
    placed = (
        jnp.zeros((row_count, gene_rows.shape[1]), jnp.float32)
        .at[local_index]
        .set(arrived.astype(jnp.float32), mode="drop")
    )
    marked = jnp.zeros((row_count,), jnp.int32).at[local_index].set(1, mode="drop")
    filled = jnp.where(marked[:, None] == 1, placed, zero_embed.astype(jnp.float32)[None, :])
    return (gene_rows.astype(jnp.float32) + filled).astype(jnp.bfloat16)


def project_heads(normed, qkv_weight):
    projected = jnp.dot(normed, qkv_weight, preferred_element_type=jnp.float32)
    row_count = projected.shape[0]
    model_width = qkv_weight.shape[0]
    query_raw = projected[:, :model_width].reshape(row_count, HEADS, HEAD)
    key_raw = projected[:, model_width : 2 * model_width].reshape(row_count, HEADS, HEAD)
    value_raw = projected[:, 2 * model_width :].reshape(row_count, HEADS, HEAD)
    return (query_raw, key_raw, value_raw)


def summarize(key_feat, value_raw):
    summary = jnp.einsum("ghj,ghe->hje", key_feat, value_raw, precision=highest)
    return (summary, jnp.sum(key_feat, axis=0))


def attend(query_feat, summary, key_total):
    numerator = jnp.einsum("ghj,hje->ghe", query_feat, summary, precision=highest)
    denominator = jnp.einsum("ghj,hj->gh", query_feat, key_total, precision=highest)
    return (numerator / denominator[..., None], denominator)


def readout_pass(gene_input, attention, proj_weight, readout):
    attended = attention.reshape(attention.shape[0], -1).astype(jnp.bfloat16)
    hidden_out = gene_input.astype(jnp.float32) + jnp.dot(
        attended, proj_weight, preferred_element_type=jnp.float32
    )
    return jnp.sum(hidden_out * readout[None, :], axis=1)


def back_to_attention(residual_grad, readout, proj_weight):
    hidden_grad = (residual_grad[:, None] * readout[None, :]).astype(jnp.bfloat16)
    grad_attn = lax.dot_general(
        hidden_grad, proj_weight, (((1,), (1,)), ((), ())), preferred_element_type=jnp.float32
    )
    return grad_attn.reshape(grad_attn.shape[0], HEADS, HEAD)


def attention_grads(grad_attn, attention, denominator, summary, key_total, query_feat):
    grad_numer = grad_attn / denominator[..., None]
    grad_denom = -jnp.sum(grad_attn * attention, axis=-1) / denominator
    grad_qfeat = (
        jnp.einsum("ghe,hje->ghj", grad_numer, summary, precision=highest)
        + grad_denom[..., None] * key_total[None]
    )
    part_summary = jnp.einsum("ghj,ghe->hje", query_feat, grad_numer, precision=highest)
    part_total = jnp.einsum("ghj,gh->hj", query_feat, grad_denom, precision=highest)
    return (grad_qfeat, part_summary, part_total)


def key_value_grads(grad_summary, grad_total, key_feat, value_raw):
    grad_kfeat = (
        jnp.einsum("ghe,hje->ghj", value_raw, grad_summary, precision=highest) + grad_total[None]
    )
    grad_value = jnp.einsum("ghj,hje->ghe", key_feat, grad_summary, precision=highest)
    return (grad_kfeat, grad_value)


def input_grads(query_raw, key_raw, grad_qfeat, grad_kfeat, grad_value):
    row_count = query_raw.shape[0]
    grad_query = jax.vjp(featurize, query_raw)[1](grad_qfeat)[0]
    grad_key = jax.vjp(featurize, key_raw)[1](grad_kfeat)[0]
    joined = jnp.concatenate(
        [
            grad_query.reshape(row_count, -1),
            grad_key.reshape(row_count, -1),
            grad_value.reshape(row_count, -1),
        ],
        axis=1,
    )
    return joined.astype(jnp.bfloat16)


def body(
    gene_ids,
    counts,
    values,
    lengths,
    bin_edges,
    bin_table,
    value_weight,
    in_weight,
    out_weight,
    gene_table,
    zero_embed,
    qkv_weight,
    proj_weight,
    readout,
    targets,
):
    ctx_count = lax.axis_size("ctx")
    slot_count = gene_ids.shape[1]
    gene_count = gene_table.shape[0]
    capacity = slot_count // ctx_count
    position = lax.axis_index("ctx") * slot_count + jnp.arange(slot_count, dtype=jnp.int32)
    live_slot = position < lengths[0]
    gene_row = gene_ids[0]
    target_range = gene_row // gene_count
    sort_order = jnp.argsort(target_range, stable=True)
    local_offset = jnp.where(live_slot, gene_row - target_range * gene_count, gene_count)[
        sort_order
    ]
    cell_edges = bin_edges[0]
    packed = jnp.stack([counts[0][sort_order], local_offset], axis=0).reshape(
        2, ctx_count, capacity
    )
    moved_values, moved_ints = (
        lax.all_to_all(
            values[0][sort_order].reshape(1, ctx_count, capacity),
            "ctx",
            split_axis=1,
            concat_axis=1,
            tiled=True,
        ),
        lax.all_to_all(packed, "ctx", split_axis=1, concat_axis=1, tiled=True),
    )
    arrived_index = moved_ints[1].reshape(slot_count)
    arrived = encode(
        moved_ints[0].reshape(slot_count),
        moved_values.reshape(slot_count),
        cell_edges,
        bin_table,
        value_weight,
        in_weight,
        out_weight,
    )
    gene_input = assemble(gene_table, arrived_index, arrived, zero_embed)
    normed = rms_round(gene_input.astype(jnp.float32))
    query_raw, key_raw, value_raw = project_heads(normed, qkv_weight)
    query_feat = featurize(query_raw)
    key_feat = featurize(key_raw)
    part_summary, part_total = summarize(key_feat, value_raw)
    summary, key_total = lax.psum((part_summary, part_total), "ctx")
    attention, denominator = attend(query_feat, summary, key_total)
    predicted = readout_pass(gene_input, attention, proj_weight, readout)
    grad_scale = 1.0 / math.sqrt(gene_count * ctx_count * lax.axis_size("dp"))
    residual_grad = (predicted - targets[0]) * grad_scale
    grad_attn = back_to_attention(residual_grad, readout, proj_weight)
    grad_qfeat, part_gsummary, part_gtotal = attention_grads(
        grad_attn, attention, denominator, summary, key_total, query_feat
    )
    grad_summary, grad_total = lax.psum((part_gsummary, part_gtotal), "ctx")
    grad_kfeat, grad_value = key_value_grads(grad_summary, grad_total, key_feat, value_raw)
    grad_rows = input_grads(query_raw, key_raw, grad_qfeat, grad_kfeat, grad_value)
    row_share = lax.psum_scatter(
        lax.dot_general(
            normed, grad_rows, (((0,), (0,)), ((), ())), preferred_element_type=jnp.float32
        ),
        "dp",
        scatter_dimension=0,
        tiled=True,
    )
    grad_qkv = lax.psum_scatter(row_share, "ctx", scatter_dimension=1, tiled=True)
    return (predicted[None, :], grad_qkv)


def solution(mesh):
    return jax.shard_map(
        body,
        mesh=mesh,
        in_specs=(
            P("dp", "ctx"),
            P("dp", "ctx"),
            P("dp", "ctx"),
            P("dp"),
            P("dp", None),
            P(),
            P(),
            P(None, "dp"),
            P("dp", None),
            P("ctx", None),
            P(),
            P(),
            P(),
            P(),
            P("dp", "ctx"),
        ),
        out_specs=(P("dp", "ctx"), P("dp", "ctx")),
        check_vma=False,
    )
```

profile of v0, /device:TPU:0, one launch (start us, length us, event | category | flops | bytes accessed | tf_op | source)
XLA Modules:
  0.0 322.8 jit_solution(3464682127952987168)
XLA Ops:
  7.2 0.7 all-gather.3.cloned.1.call-update
  8.0 0.7 all-gather.5.cloned.1.call-update
  9.3 0.7 compare_select_fusion.2
  10.0 2.5 sort.17
  12.5 1.6 gather_fusion.2
  14.1 0.7 reshape.136
  14.8 5.2 %all-to-all-start.1 = ((f32[1,4,32]{2,0,1:T(1,128)}), f32[1,4,32]{2,0,1:T(1,128)S(1)}, u32[]{:S(2)}, u32[]{:S(2)}) async-start(f32[1,4,32]{2,0,1:T(1,128)} %bitcast.6), calls=%async_computation.1 | async-start | bytes 4096 | tf_op jit(solution)/shard_map/all_to_all | solution.py:172
  20.0 1.2 gather_fusion.1
  21.3 1.6 gather_fusion
  23.0 0.6 copy.45
  23.6 1.0 all-to-all-done.1
  24.5 3.2 %all-to-all-start = ((s32[2,4,32]{2,0,1:T(2,128)}), s32[2,4,32]{2,0,1:T(2,128)S(1)}, u32[]{:S(2)}, u32[]{:S(2)}) async-start(s32[2,4,32]{2,0,1:T(2,128)} %copy.45), calls=%async_computation | async-start | bytes 8192 | tf_op jit(solution)/shard_map/all_to_all | solution.py:179
  27.8 0.7 convert_element_type.48
  28.5 0.7 reduce.4
  29.3 0.5 broadcast.180
  29.8 0.7 reduce.13
  30.4 0.1 mul.211
  30.5 1.9 all-to-all-done
  32.6 1.0 scatter_custom_fusion
  33.6 0.7 convert_reduce_fusion
  34.4 1.1 multiply_reduce_fusion.5
  35.5 4.0 %all-gather.3.cloned.1.call-done = bf16[384,2048]{1,0:T(8,128)(2,1)} async-done(((bf16[384,256]{1,0:T(8,128)(2,1)}), bf16[384,2048]{1,0:T(8,128)(2,1)}) %all-gather.3.cloned.1.call-update) | async-done | bytes 1572880 | tf_op jit(solution)/shard_map/all_gather | solution.py:42
  39.5 25.9 %all-gather.5.cloned.1.call-done = bf16[2048,384]{1,0:T(8,128)(2,1)} async-done(((bf16[256,384]{1,0:T(8,128)(2,1)}), bf16[2048,384]{1,0:T(8,128)(2,1)}) %all-gather.5.cloned.1.call-update) | async-done | bytes 1572880 | tf_op jit(solution)/shard_map/all_gather | solution.py:48
  65.4 2.6 fusion.33
  68.1 3.4 %scatter_custom_fusion.1 = f32[2408,384]{1,0:T(8,128)} fusion(s32[128]{0:T(128)S(1)} %fusion.48, f32[128,384]{1,0:T(8,128)S(1)} %fusion.33, f32[]{:T(128)} %constant.20.clone.1), kind=kCustom, calls=%fused_computation.54 | custom fusion | bytes 3698692 | tf_op jit(solution)/shard_map/scatter | solution.py:59
  71.5 3.7 %fusion.14 = (f32[2408]{0:T(1024)S(1)}, bf16[2408,384]{1,0:T(8,128)(2,1)S(1)}) fusion(f32[2408,384]{1,0:T(8,128)} %scatter_custom_fusion.1, f32[384]{0:T(512)S(1)} %convert_element_type.48, pred[2408]{0:T(1024)(128)(4,1)S(1)} %broadcast_compare_fusion, bf16[2408,384]{1,0:T(8,128)(2,1)} %param.24), kind=kLoop, calls=%fused_computation.35 | loop fusion | flops 6470296 | bytes 7410952 | tf_op jit(solution)/shard_map/reduce_sum | solution.py:23
  75.2 3.4 %fusion.35 = f32[2408,1152]{1,0:T(8,128)S(1)} fusion(bf16[384,1152]{1,0:T(8,128)(2,1)S(1)} %copy-done, bf16[2408,384]{1,0:T(8,128)(2,1)S(1)} %get-tuple-element.7, f32[2408]{0:T(1024)S(1)} %add_rsqrt_fusion), kind=kOutput, calls=%fused_computation.62 | convolution fusion | flops 2133218304 | bytes 13839776 | tf_op jit(solution)/shard_map/dot_general | solution.py:67
  78.6 4.1 %copy-done.6 = f32[2408,1152]{1,0:T(8,128)} copy-done((f32[2408,1152]{1,0:T(8,128)}, f32[2408,1152]{1,0:T(8,128)S(1)}, u32[]{:S(2)}) %copy-start.6) | copy-done | bytes 11096088
  82.7 2.0 slice.28
  84.8 5.3 %copy.47 = f32[2408,384]{0,1:T(8,128)} copy(f32[2408,384]{1,0:T(8,128)} %slice.28) | data formatting | bytes 7397376 | tf_op jit(solution)/shard_map/slice | solution.py:71
  90.1 2.4 multiply_reduce_fusion.4
  92.6 2.1 mul.225
  94.7 5.4 %copy.51 = f32[2408,384]{1,0:T(8,128)} copy(f32[2408,384]{0,1:T(8,128)} %bitcast.92) | data formatting | bytes 7397376 | tf_op jit(solution)/shard_map/mul | solution.py:19
  100.1 8.9 %exponential_reduce_fusion = (f32[384]{0:T(512)S(1)}, f32[2408,384]{1,0:T(8,128)}, f32[2408,384]{1,0:T(8,128)}) fusion(f32[2408,384]{1,0:T(8,128)} %copy.51, f32[2408,1152]{1,0:T(8,128)} %copy-done.6), kind=kLoop, calls=%fused_computation.38 | loop fusion | flops 1848960 | bytes 22193664 | tf_op jit(solution)/shard_map/reduce_sum | solution.py:78
  109.0 5.3 %copy.48 = f32[2408,384]{0,1:T(8,128)} copy(f32[2408,384]{1,0:T(8,128)} %get-tuple-element.12) | data formatting | bytes 7397376 | tf_op jit(solution)/shard_map/slice | solution.py:72
  114.3 7.9 %fusion.16 = f32[6,64,64]{2,1,0:T(8,128)} fusion(f32[2408,6,64]{0,2,1:T(8,128)} %bitcast.87, f32[2408,6,64]{0,2,1:T(8,128)} %bitcast.76, f32[2408,6]{0,1:T(8,128)S(1)} %get-tuple-element.16), kind=kOutput, calls=%fused_computation.40 | convolution fusion | flops 711072768 | bytes 7553472 | tf_op jit(solution)/shard_map/ghj,ghe->hje/dot_general | solution.py:77
  122.3 5.3 %copy.49 = f32[2408,384]{0,1:T(8,128)} copy(f32[2408,384]{1,0:T(8,128)} %get-tuple-element.11) | data formatting | bytes 7397376 | tf_op jit(solution)/shard_map/slice | solution.py:70
  127.6 2.4 multiply_reduce_fusion.3
  130.1 10.0 %psum.29 = f32[6,64]{1,0:T(8,128)S(1)} all-reduce(f32[6,64]{1,0:T(8,128)S(1)} %reduce_sum.114), channel_id=1, replica_groups=mesh['dp'=8,'ctx'=4] {'ctx'}, use_global_device_ids=true, to_apply=%region_10.11 | all-reduce | flops 384 | bytes 3072 | tf_op jit(solution)/shard_map/psum | solution.py:197
  140.1 4.3 %fusion.19 = f32[6,1,2408]{2,1,0:T(1,128)S(1)} fusion(f32[2408,6,64]{0,2,1:T(8,128)} %bitcast.81, f32[2408,6]{0,1:T(8,128)S(1)} %get-tuple-element.14, f32[6,64,1]{1,0,2:T(8,128)S(1)} %bitcast.103), kind=kOutput, calls=%fused_computation.43 | convolution fusion | flops 12020736 | bytes 3815808 | tf_op jit(solution)/shard_map/ghj,hj->gh/dot_general | solution.py:83
  144.4 19.9 %all-reduce.3.cloned.1.call-done = f32[6,64,64]{2,1,0:T(8,128)} async-done(((f32[6,64,64]{2,1,0:T(8,128)}), f32[6,64,64]{2,1,0:T(8,128)}) %all-reduce.3.cloned.1.call-update) | async-done | bytes 98320 | tf_op jit(solution)/shard_map/psum | solution.py:197
  164.4 7.6 %fusion.51 = (bf16[2408,6,64]{0,2,1:T(8,128)(2,1)S(1)}, f32[2408,6,64]{0,2,1:T(8,128)}) fusion(f32[2408,6]{0,1:T(8,128)S(1)} %bitcast.99, f32[6,64,64]{2,1,0:T(8,128)} %all-reduce.3.cloned.1.call-done, f32[2408,6,64]{0,2,1:T(8,128)} %bitcast.82, f32[2408,6]{0,1:T(8,128)S(1)} %get-tuple-element.14), kind=kOutput, calls=%fused_computation.104 | convolution fusion | flops 712922112 | bytes 9460608 | tf_op jit(solution)/shard_map/ghj,hje->ghe/dot_general | solution.py:82
  172.0 1.6 fusion.31
  173.5 1.3 fusion.26
  174.8 1.8 copy-done.7
  176.6 5.1 %fusion.18 = f32[6,64,64]{2,1,0:T(8,128)} fusion(f32[2408,6,64]{0,2,1:T(8,128)S(1)} %bitcast.84, f32[2408,6]{0,1:T(8,128)S(1)} %get-tuple-element.14, f32[2408,6,64]{0,2,1:T(8,128)S(1)} %bitcast.89, f32[2408,6]{0,1:T(8,128)S(1)} %bitcast.100), kind=kOutput, calls=%fused_computation.42 | convolution fusion | flops 711997440 | bytes 7611264 | tf_op jit(solution)/shard_map/ghj,ghe->hje/dot_general | solution.py:110
  181.7 3.8 %multiply_reduce_fusion.2 = f32[2408,6]{0,1:T(8,128)S(1)} fusion(f32[2408,6,64]{0,2,1:T(8,128)} %bitcast.90, f32[2408,6,64]{0,2,1:T(8,128)} %get-tuple-element.20), kind=kLoop, calls=%fused_computation.30 | loop fusion | flops 1834896 | bytes 7455168 | tf_op jit(solution)/shard_map/reduce_sum | solution.py:105
  185.6 0.4 copy-done.4
  185.9 1.1 copy-done.8
  187.1 6.2 %multiply_reduce_fusion.1 = (f32[2408,6]{0,1:T(8,128)S(1)}, f32[2408,6,64]{0,2,1:T(8,128)}) fusion(f32[2408,6,64]{0,2,1:T(8,128)S(1)} %bitcast.85, f32[2408,6]{0,1:T(8,128)S(1)} %get-tuple-element.14, f32[6,64]{1,0:T(8,128)S(1)} %psum.29, f32[2408,6]{0,1:T(8,128)S(1)} %negate_divide_fusion, f32[6,64,64]{2,1,0:T(8,128)S(1)} %copy-done.13, ...), kind=kOutput, calls=%fused_computation.29 | convolution fusion | flops 717531008 | bytes 11427072 | tf_op jit(solution)/shard_map/ghe,hje->ghj/dot_general | solution.py:107
  193.4 5.4 %fusion.12 = bf16[2408,6,64]{0,2,1:T(8,128)(2,1)} fusion(f32[2408,6,64]{0,2,1:T(8,128)} %bitcast.83, f32[2408,6,64]{0,2,1:T(8,128)} %get-tuple-element.24, f32[2408,6]{0,1:T(8,128)S(1)} %multiply_multiply_fusion.1, f32[2408,6]{0,1:T(8,128)S(1)} %get-tuple-element.13), kind=kLoop, calls=%fused_computation.26 | loop fusion | flops 5548032 | bytes 9362304 | tf_op jit(solution)/shard_map/convert.6
  198.8 3.8 %fusion.17 = f32[6,1,64]{2,1,0:T(1,128)S(1)} fusion(f32[2408,6,64]{0,2,1:T(8,128)S(1)} %bitcast.86, f32[2408,6]{0,1:T(8,128)S(1)} %get-tuple-element.14, f32[2408,6,1]{0,1,2:T(8,128)S(1)} %bitcast.97), kind=kOutput, calls=%fused_computation.41 | convolution fusion | flops 12020736 | bytes 3815808 | tf_op jit(solution)/shard_map/ghj,gh->hj/dot_general | solution.py:111
  202.5 9.2 %psum.31 = f32[6,64]{1,0:T(8,128)S(1)} all-reduce(f32[6,64]{1,0:T(8,128)S(1)} %bitcast.102), channel_id=1, replica_groups=mesh['dp'=8,'ctx'=4] {'ctx'}, use_global_device_ids=true, to_apply=%region_15.16 | all-reduce | flops 384 | bytes 3072 | tf_op jit(solution)/shard_map/psum | solution.py:206
  211.7 24.2 %all-reduce.5.cloned.1.call-done = f32[6,64,64]{2,1,0:T(8,128)} async-done(((f32[6,64,64]{2,1,0:T(8,128)}), f32[6,64,64]{2,1,0:T(8,128)}) %all-reduce.5.cloned.1.call-update) | async-done | bytes 98320 | tf_op jit(solution)/shard_map/psum | solution.py:206
  235.9 7.8 %multiply_reduce_fusion = (f32[2408,6]{0,1:T(8,128)S(1)}, f32[2408,6,64]{0,2,1:T(8,128)S(1)}) fusion(f32[2408,6,64]{0,2,1:T(8,128)} %bitcast.77, f32[2408,6]{0,1:T(8,128)S(1)} %get-tuple-element.16, f32[6,64]{1,0:T(8,128)S(1)} %psum.31, f32[6,64,64]{2,1,0:T(8,128)} %all-reduce.5.cloned.1.call-done, f32[2408,6,64]{0,2,1:T(8,128)} %bitcast.88), kind=kOutput, calls=%fused_computation.28 | convolution fusion | flops 715681664 | bytes 11311488 | tf_op jit(solution)/shard_map/ghe,hje->ghj/dot_general | solution.py:117
  243.8 0.7 fusion.13
  244.5 0.2 copy-done.10
  244.7 3.5 %convolution_convert_fusion = bf16[6,64,2408]{2,1,0:T(8,128)(2,1)S(1)} fusion(f32[6,64,64]{2,1,0:T(8,128)S(1)} %copy-done.10, f32[2408,6,64]{0,2,1:T(8,128)S(1)} %bitcast.79, f32[2408,6]{0,1:T(8,128)S(1)} %get-tuple-element.16), kind=kOutput, calls=%fused_computation.24 | convolution fusion | flops 711997440 | bytes 5704128 | tf_op jit(solution)/shard_map/ghj,hje->ghe/dot_general | solution.py:119
  248.3 4.5 %fusion = f32[384,1152]{1,0:T(8,128)} fusion(bf16[2408,384]{0,1:T(8,128)(2,1)S(1)} %bitcast.94, bf16[2408,384]{0,1:T(8,128)(2,1)S(1)} %bitcast.96, bf16[2408,384]{0,1:T(8,128)(2,1)S(1)} %bitcast.95, bf16[2408,384]{1,0:T(8,128)(2,1)S(1)} %get-tuple-element.7, f32[2408]{0:T(1024)S(1)} %add_rsqrt_fusion), kind=kOutput, calls=%fused_computation.5 | convolution fusion | flops 2149862400 | bytes 9176480 | tf_op jit(solution)/shard_map/dot_general | solution.py:210
  252.9 35.1 %reduce-scatter.5.cloned.1.call-done = f32[48,1152]{1,0:T(8,128)} async-done(((f32[384,1152]{1,0:T(8,128)}), f32[48,1152]{1,0:T(8,128)}) %reduce-scatter.5.cloned.1.call-update) | async-done | bytes 221200 | tf_op jit(solution)/shard_map/reduce_scatter | solution.py:209
  288.0 2.0 copy.61
  290.0 0.6 broadcast_in_dim.35
  290.6 23.3 %reduce-scatter.7.cloned.1.call-done = f32[288,48]{1,0:T(8,128)} async-done(((f32[1152,48]{1,0:T(8,128)}), f32[288,48]{1,0:T(8,128)}) %reduce-scatter.7.cloned.1.call-update) | async-done | bytes 55312
  313.9 1.7 copy.62
  (56 shorter events, 1.0 us)
Async XLA Ops:
  7.2 68.0 %copy-start = (bf16[384,1152]{1,0:T(8,128)(2,1)S(1)}, bf16[384,1152]{1,0:T(8,128)(2,1)}, u32[]{:S(2)}) copy-start(bf16[384,1152]{1,0:T(8,128)(2,1)} %param.26) | copy-start | bytes 2654212
  7.2 32.3 %all-gather.3.cloned.1.call-start = ((), (), s32[]{:S(2)}) async-start(), calls=%async_computation.4 | async-start | bytes 1769472 | tf_op jit(solution)/shard_map/all_gather | solution.py:42
  7.9 57.5 %all-gather.5.cloned.1.call-start = ((), (), s32[]{:S(2)}) async-start(), calls=%async_computation.5 | async-start | bytes 1769472 | tf_op jit(solution)/shard_map/all_gather | solution.py:48
  14.8 9.7 %all-to-all-start.1 = ((f32[1,4,32]{2,0,1:T(1,128)}), f32[1,4,32]{2,0,1:T(1,128)S(1)}, u32[]{:S(2)}, u32[]{:S(2)}) async-start(f32[1,4,32]{2,0,1:T(1,128)} %bitcast.6), calls=%async_computation.1 | async-start | bytes 4096 | tf_op jit(solution)/shard_map/all_to_all | solution.py:172
  24.5 7.9 %all-to-all-start = ((s32[2,4,32]{2,0,1:T(2,128)}), s32[2,4,32]{2,0,1:T(2,128)S(1)}, u32[]{:S(2)}, u32[]{:S(2)}) async-start(s32[2,4,32]{2,0,1:T(2,128)} %copy.45), calls=%async_computation | async-start | bytes 8192 | tf_op jit(solution)/shard_map/all_to_all | solution.py:179
  27.8 136.6 %all-reduce.3.cloned.1.call-start = ((), (), s32[]{:S(2)}) async-start(), calls=%async_computation.6 | async-start | bytes 393216 | tf_op jit(solution)/shard_map/psum | solution.py:197
  78.6 4.1 %copy-start.6 = (f32[2408,1152]{1,0:T(8,128)}, f32[2408,1152]{1,0:T(8,128)S(1)}, u32[]{:S(2)}) copy-start(f32[2408,1152]{1,0:T(8,128)S(1)} %fusion.35) | copy-start | bytes 33288196
  122.2 113.7 %all-reduce.5.cloned.1.call-start = ((), (), s32[]{:S(2)}) async-start(), calls=%async_computation.7 | async-start | bytes 393216 | tf_op jit(solution)/shard_map/psum | solution.py:206
  164.3 7.6 %copy-start.11 = (bf16[384,384]{1,0:T(8,128)(2,1)S(1)}, bf16[384,384]{1,0:T(8,128)(2,1)}, u32[]{:S(2)}) copy-start(bf16[384,384]{1,0:T(8,128)(2,1)} %param.27) | copy-start | bytes 884740
  164.4 7.6 %copy-start.12 = (f32[384]{0:T(512)S(1)}, f32[384]{0:T(512)}, u32[]{:S(2)}) copy-start(f32[384]{0:T(512)} %param.28) | copy-start | bytes 4612
  173.5 3.1 copy-start.3
  174.8 1.8 copy-start.7
  181.7 4.2 %copy-start.4 = (f32[2408,384]{0,1:T(8,128)S(1)}, f32[2408,384]{0,1:T(8,128)}, u32[]{:S(2)}) copy-start(f32[2408,384]{0,1:T(8,128)} %copy.49) | copy-start | bytes 11096068
  181.7 5.4 %copy-start.8 = (f32[2408,384]{0,1:T(8,128)S(1)}, f32[2408,384]{0,1:T(8,128)}, u32[]{:S(2)}) copy-start(f32[2408,384]{0,1:T(8,128)} %copy-done.7) | copy-start | bytes 11096068
  181.7 5.4 %copy-start.13 = (f32[6,64,64]{2,1,0:T(8,128)S(1)}, f32[6,64,64]{2,1,0:T(8,128)}, u32[]{:S(2)}) copy-start(f32[6,64,64]{2,1,0:T(8,128)} %all-reduce.3.cloned.1.call-done) | copy-start | bytes 294916
  193.3 94.7 %reduce-scatter.5.cloned.1.call-start = ((), (), s32[]{:S(2)}) async-start(), calls=%async_computation.8 | async-start | bytes 1990656 | tf_op jit(solution)/shard_map/reduce_scatter | solution.py:209
  193.4 5.4 %copy-start.5 = (f32[2408,384]{0,1:T(8,128)S(1)}, f32[2408,384]{0,1:T(8,128)}, u32[]{:S(2)}) copy-start(f32[2408,384]{0,1:T(8,128)} %copy.49) | copy-start | bytes 11096068
  235.9 7.9 %copy-start.2 = (f32[2408,384]{0,1:T(8,128)S(1)}, f32[2408,384]{0,1:T(8,128)}, u32[]{:S(2)}) copy-start(f32[2408,384]{0,1:T(8,128)} %copy.47) | copy-start | bytes 11096068
  243.8 0.9 copy-start.10
  244.7 3.6 %copy-start.9 = (bf16[2408,6,64]{0,2,1:T(8,128)(2,1)S(1)}, bf16[2408,6,64]{0,2,1:T(8,128)(2,1)}, u32[]{:S(2)}) copy-start(bf16[2408,6,64]{0,2,1:T(8,128)(2,1)} %fusion.12) | copy-start | bytes 5548036
  248.3 67.3 %copy-start.1 = (bf16[384,1152]{1,0:T(8,128)(2,1)S(1)}, bf16[384,1152]{1,0:T(8,128)(2,1)}, u32[]{:S(2)}) copy-start(bf16[384,1152]{1,0:T(8,128)(2,1)} %param.26) | copy-start | bytes 2654212
  252.9 61.0 %reduce-scatter.7.cloned.1.call-start = ((), (), s32[]{:S(2)}) async-start(), calls=%async_computation.9 | async-start | bytes 737280
Sparse Core Ops, SparseCore 0:
  9.6 29.8 all-gather.2
  41.2 24.1 all-gather.4
  122.3 41.9 all-reduce.2
  193.4 42.4 all-reduce.4
  253.0 34.9 reduce-scatter.4
  290.7 23.1 reduce-scatter.6
where the time goes:
time: 327 us; the launch traced here: 323 us
  waiting for transfers between devices  137 us (42%)
  matrix products  60.6 us (19%)
  local copies, waits for them, and re-layouts  48.6 us (15%)
  other arithmetic  33.6 us (10%)
  blocking collectives  19.1 us (6%)
  between operations  15.5 us (5%)
  starting transfers between devices  8.65 us (3%)
    reduce_scatter x1, waiting for transfers between devices, body(): lax.psum_scatter(lax.dot_general(normed, grad_rows, (((0,), (0,)), ((), (...  35.1 us
    all_gather x1, waiting for transfers between devices, encode(): lax.all_gather(out_weight, 'dp', axis=0, tiled=True)  25.9 us
    unnamed x7, waiting for transfers between devices  24.7 us
    psum x1, waiting for transfers between devices, body(): grad_summary, grad_total = lax.psum((part_gsummary, part_gtotal), 'ctx')  24.2 us
    psum x1, waiting for transfers between devices, body(): summary, key_total = lax.psum((part_summary, part_total), 'ctx')  19.9 us
    unnamed x30, local copies, waits for them, and re-layouts  11.3 us
    psum x1, blocking collectives, body(): summary, key_total = lax.psum((part_summary, part_total), 'ctx')  9.96 us
    psum x1, blocking collectives, body(): grad_summary, grad_total = lax.psum((part_gsummary, part_gtotal), 'ctx')  9.15 us
  transfers between devices with their start and end apart: 8, of which 8 were waited for; matrix products, arithmetic and copies ran while one was open for 11% of the time, Pallas kernels for 0%

commit v1 on v0

--- a/solution.py
+++ b/solution.py
@@ -1,12 +1,16 @@
+import functools
 import math
 
 import jax
 import jax.numpy as jnp
 from jax import lax
+from jax.experimental import pallas as pl
+from jax.experimental.pallas import tpu as pltpu
 from jax.sharding import PartitionSpec as P
 
 HEAD = 64
 HEADS = 6
+CHUNKS = 8
 
 
 feature_scale = 2.5
@@ -218,9 +222,535 @@
     return (predicted[None, :], grad_qkv)
 
 
+MESH = pl.DeviceIdType.MESH
+F32 = jnp.float32
+BF16 = jnp.bfloat16
+
+
+def mm(left, right):
+    return jnp.dot(left, right, preferred_element_type=F32)
+
+
+def split(x):
+    high = x.astype(BF16)
+    return high, (x - high.astype(F32)).astype(BF16)
+
+
+def head_sum(x, ones):
+    high, low = split(x)
+    parts = []
+    for start in range(0, x.shape[1], 256):
+        width = min(256, x.shape[1] - start)
+        block = ones[:width, :width]
+        parts.append(
+            mm(high[:, start : start + width], block) + mm(low[:, start : start + width], block)
+        )
+    return jnp.concatenate(parts, axis=1)
+
+
+def rms(x):
+    return x * lax.rsqrt(jnp.mean(x * x, axis=-1, keepdims=True) + norm_eps)
+
+
+def lanes_to_rows(row, rows=128):
+    return jnp.transpose(jnp.broadcast_to(row, (rows, row.shape[1])))
+
+
+def send(src, dst, sems, index_send, index_recv, device):
+    copy = pltpu.make_async_remote_copy(
+        src_ref=src,
+        dst_ref=dst,
+        send_sem=sems[0].at[index_send],
+        recv_sem=sems[1].at[index_recv],
+        device_id=device,
+        device_id_type=MESH,
+    )
+    copy.start()
+    return copy
+
+
+def kernel(
+    gene_count,
+    chunk,
+    ids_ref,
+    counts_ref,
+    values_ref,
+    lengths_ref,
+    edges_ref,
+    table_ref,
+    vweight_ref,
+    in_ref,
+    out_ref,
+    gene_ref,
+    zero_ref,
+    qkv_ref,
+    proj_ref,
+    readout_ref,
+    targets_ref,
+    pred_ref,
+    grad_ref,
+    table,
+    ones,
+    wvw_hi,
+    wvw_lo,
+    slots,
+    tokens,
+    ff_send,
+    ff_recv,
+    normed,
+    unit,
+    inverse,
+    vwx,
+    rows,
+    base_dot,
+    target_x,
+    keep_x,
+    pred_x,
+    sums1,
+    sums2,
+    grads,
+    core_recv,
+    z_send,
+    z_recv,
+    part,
+    ctx_recv,
+    slot_s,
+    slot_r,
+    tok_s,
+    tok_r,
+    ff_s,
+    ff_r,
+    one_s,
+    one_r,
+    two_s,
+    two_r,
+    core_s,
+    core_r,
+    z_s,
+    z_r,
+    last_s,
+    last_r,
+):
+    ctx = lax.axis_index("ctx")
+    dp = lax.axis_index("dp")
+    ctx_n = slots.shape[0]
+    dp_n = tokens.shape[0]
+    padded = gene_ref.shape[0]
+    width = gene_ref.shape[1]
+    tok_n = ids_ref.shape[1]
+    cap = tok_n // ctx_n
+
+    barrier = pltpu.get_barrier_semaphore()
+    for k in range(1, ctx_n):
+        pl.semaphore_signal(
+            barrier, inc=1, device_id={"ctx": lax.rem(ctx + k, ctx_n)}, device_id_type=MESH
+        )
+    for k in range(1, dp_n):
+        pl.semaphore_signal(
+            barrier, inc=1, device_id={"dp": lax.rem(dp + k, dp_n)}, device_id_type=MESH
+        )
+
+    counts = counts_ref[...]
+    binned = jnp.zeros(counts.shape, F32)
+    for j in range(edges_ref.shape[1]):
+        binned = binned + jnp.where(counts >= edges_ref[0, j], 1.0, 0.0)
+    lane = lax.broadcasted_iota(jnp.int32, (1, tok_n), 1)
+    live = (ctx * tok_n + lane) < lengths_ref[0]
+    gene_f = jnp.where(live, ids_ref[...].astype(F32), -1.0)
+    sub = lax.broadcasted_iota(jnp.int32, (8, tok_n), 0)
+    slots[ctx] = jnp.where(
+        sub == 0, gene_f, jnp.where(sub == 1, binned, jnp.where(sub == 2, values_ref[...], 0.0))
+    )
+    pl.semaphore_wait(barrier, ctx_n + dp_n - 2)
+    copies = []
+    for k in range(1, ctx_n):
+        copies.append(
+            send(
+                slots.at[ctx],
+                slots.at[ctx],
+                (slot_s, slot_r),
+                k,
+                k,
+                {"ctx": lax.rem(ctx + k, ctx_n)},
+            )
+        )
+
+    hrow = lax.broadcasted_iota(jnp.int32, (256, 256), 0) // HEAD
+    hcol = lax.broadcasted_iota(jnp.int32, (256, 256), 1) // HEAD
+    ones[...] = jnp.where(hrow == hcol, 1.0, 0.0).astype(BF16)
+    readout = readout_ref[...]
+    w_col = jnp.sum(proj_ref[...].astype(F32) * readout, axis=1, keepdims=True)
+    w_row = jnp.transpose(jnp.broadcast_to(w_col, (width, 128)))[0:1, :]
+    v_dot = head_sum(qkv_ref[:, 2 * width :].astype(F32) * w_row, ones)
+    v_high, v_low = split(v_dot)
+    wvw_hi[...] = v_high
+    wvw_lo[...] = v_low
+    table[...] = jnp.zeros_like(table)
+    table[0 : table_ref.shape[0], :] = table_ref[...].astype(F32)
+    table_b = table[...].astype(BF16)
+    target_x[0:padded, :] = lanes_to_rows(targets_ref[...])
+    for copy in copies:
+        copy.wait()
+
+    first = (ctx * gene_count).astype(F32)
+    upper = jnp.where(
+        lax.broadcasted_iota(jnp.int32, (tok_n, tok_n), 0)
+        < lax.broadcasted_iota(jnp.int32, (tok_n, tok_n), 1),
+        1.0,
+        0.0,
+    ).astype(BF16)
+    place = lax.broadcasted_iota(jnp.int32, (cap, tok_n), 0).astype(F32)
+    idx_parts, bin_parts, val_parts = [], [], []
+    for s in range(ctx_n):
+        held = slots[s]
+        local = held - first
+        inside = (held >= first) & (local < gene_count)
+        inside = jnp.where(inside, 1.0, 0.0)
+        rank = mm(inside.astype(BF16), upper)
+        chosen = (inside[0:1] > 0.5) & (rank[0:1] == place)
+        idx_parts.append(jnp.sum(jnp.where(chosen, local[0:1] + 1.0, 0.0), axis=1, keepdims=True))
+        bin_parts.append(jnp.sum(jnp.where(chosen, held[1:2], 0.0), axis=1, keepdims=True))
+        val_parts.append(jnp.sum(jnp.where(chosen, held[2:3], 0.0), axis=1, keepdims=True))
+    idx_col = jnp.concatenate(idx_parts, axis=0) - 1.0
+    bin_col = jnp.concatenate(bin_parts, axis=0)
+    val_col = jnp.concatenate(val_parts, axis=0)
+    square = lax.broadcasted_iota(jnp.int32, (tok_n, 128), 1)
+    mine = jnp.transpose(
+        jnp.where(square == 0, bin_col, jnp.where(square == 1, val_col, jnp.where(square == 2, idx_col, 0.0)))
+    )
+    tokens[dp] = mine[0:8]
+    copies = []
+    for k in range(1, dp_n):
+        copies.append(
+            send(
+                tokens.at[dp], tokens.at[dp], (tok_s, tok_r), k, k, {"dp": lax.rem(dp + k, dp_n)}
+            )
+        )
+    idx_row = mine[2:3]
+
+    gene_lane = lax.broadcasted_iota(jnp.int32, (tok_n, padded), 1).astype(F32)
+    hit = gene_lane == idx_col
+    token_base = mm(jnp.where(hit, 1.0, 0.0).astype(BF16), gene_ref[...])
+    taken = jnp.sum(jnp.where(hit, 1.0, 0.0), axis=0, keepdims=True)
+    tok_target = jnp.sum(jnp.where(hit, targets_ref[...], 0.0), axis=1, keepdims=True)
+    in_range = lax.broadcasted_iota(jnp.int32, (1, padded), 1) < gene_count
+    keep_row = jnp.where(in_range & (taken < 0.5), 1.0, 0.0)
+    keep_x[0:padded, :] = lanes_to_rows(keep_row)
+    tok_live = jnp.where(idx_col > -0.5, 1.0, 0.0)
+    keep_x[padded:, :] = jnp.broadcast_to(tok_live, (tok_n, 128))
+    target_x[padded:, :] = jnp.broadcast_to(tok_target, (tok_n, 128))
+
+    pick = lax.broadcasted_iota(jnp.int32, (tok_n, table.shape[0]), 1).astype(F32)
+
+    def embed(bin_c, val_c):
+        one_hot = jnp.where(bin_c == pick, 1.0, 0.0).astype(BF16)
+        return mm(one_hot, table_b) + val_c * vweight_ref[...]
+
+    def feed(emb):
+        pre = mm(rms(emb).astype(BF16), in_ref[...])
+        act = (pre / (1.0 + jnp.exp(-pre))).astype(BF16)
+        return mm(act, out_ref[...])
+
+    ff_copies = []
+    for k in range(1, dp_n):
+        copies[k - 1].wait()
+    for k in range(1, dp_n):
+        other = lax.rem(dp + k, dp_n)
+        got = jnp.transpose(jnp.concatenate([tokens[other]] * (128 // 8), axis=0))
+        ff_send[k] = feed(embed(got[:, 0:1], got[:, 1:2])).astype(BF16)
+        ff_copies.append(
+            send(ff_send.at[k], ff_recv.at[k], (ff_s, ff_r), k, k, {"dp": other})
+        )
+    own_emb = embed(bin_col, val_col)
+    own_mix = own_emb + feed(own_emb)
+
+    def features(start, count, gene_input):
+        at = pl.ds(start, count)
+        gi = gene_input.astype(BF16).astype(F32)
+        nb = rms(gi).astype(BF16)
+        normed[at, :] = nb
+        base_dot[at, :] = jnp.broadcast_to(
+            jnp.sum(gi * readout, axis=1, keepdims=True), (count, 128)
+        )
+        raw = mm(nb, qkv_ref[:, : 2 * width])
+        inv = lax.rsqrt(head_sum(raw * raw, ones) * (1.0 / HEAD) + norm_eps)
+        u = raw * inv
+        unit[at, :] = u
+        inverse[at, :] = inv
+        vw = mm(nb, wvw_hi[...]) + mm(nb, wvw_lo[...])
+        vwx[at, :] = vw
+        kf = jnp.exp(feature_scale * u[:, width:]) * keep_x[at, 0:1]
+        return (
+            jnp.sum(kf, axis=0, keepdims=True),
+            jnp.sum(kf * vw, axis=0, keepdims=True),
+        )
+
+    zero = zero_ref[...].astype(F32)
+    none = jnp.zeros((1, width), F32)
+
+    def first_pass(i, carry):
+        start = pl.multiple_of(i * chunk, 16)
+        a, b = features(start, chunk, gene_ref[pl.ds(start, chunk), :].astype(F32) + zero)
+        return carry[0] + a, carry[1] + b
+
+    kt, us = lax.fori_loop(0, padded // chunk, first_pass, (none, none))
+    for copy in ff_copies:
+        copy.wait()
+    for k in range(1, dp_n):
+        own_mix = own_mix + ff_recv[k].astype(F32)
+    a, b = features(padded, tok_n, token_base + own_mix.astype(BF16).astype(F32))
+    kt, us = kt + a, us + b
+
+    def over_ctx(buffer, sems, x, y):
+        row_at = lax.broadcasted_iota(jnp.int32, (8, width), 0)
+        buffer[ctx] = jnp.where(row_at == 0, x, jnp.where(row_at == 1, y, 0.0))
+        sent = []
+        for k in range(1, ctx_n):
+            sent.append(
+                send(buffer.at[ctx], buffer.at[ctx], sems, k, k, {"ctx": lax.rem(ctx + k, ctx_n)})
+            )
+        for copy in sent:
+            copy.wait()
+        total = buffer[0]
+        for s in range(1, ctx_n):
+            total = total + buffer[s]
+        return total[0:1], total[1:2]
+
+    kt, us = over_ctx(sums1, (one_s, one_r), kt, us)
+    scale = 1.0 / math.sqrt(gene_count * ctx_n * dp_n)
+
+    def query_pass(start, count, carry):
+        at = pl.ds(start, count)
+        u = unit[at, :width]
+        qf = jnp.exp(feature_scale * u)
+        den = head_sum(qf * kt, ones)
+        att = head_sum(qf * us, ones) / den
+        predicted = base_dot[at, 0:1] + jnp.sum(att, axis=1, keepdims=True) * (1.0 / HEAD)
+        pred_x[at, :] = jnp.broadcast_to(predicted, (count, 128))
+        res = (predicted - target_x[at, 0:1]) * (scale * keep_x[at, 0:1])
+        qs = qf * (res / den)
+        h = qs * (us - att * kt)
+        back = head_sum(h * u, ones) * (1.0 / HEAD)
+        rows[at, :width] = (feature_scale * inverse[at, :width] * (h - u * back)).astype(BF16)
+        return (
+            carry[0] + jnp.sum(qs, axis=0, keepdims=True),
+            carry[1] - jnp.sum(qs * att, axis=0, keepdims=True),
+        )
+
+    cs, ts = lax.fori_loop(
+        0,
+        padded // chunk,
+        lambda i, carry: query_pass(pl.multiple_of(i * chunk, 16), chunk, carry),
+        (none, none),
+    )
+    cs, ts = query_pass(padded, tok_n, (cs, ts))
+    cs, ts = over_ctx(sums2, (two_s, two_r), cs, ts)
+    pick6 = jnp.where(
+        lax.broadcasted_iota(jnp.int32, (width, 128), 0) // HEAD
+        == lax.broadcasted_iota(jnp.int32, (width, 128), 1),
+        1.0,
+        0.0,
+    ).astype(BF16)
+
+    def key_pass(start, count):
+        at = pl.ds(start, count)
+        u = unit[at, width:]
+        kf = jnp.exp(feature_scale * u) * keep_x[at, 0:1]
+        h = kf * (vwx[at, :] * cs + ts)
+        back = head_sum(h * u, ones) * (1.0 / HEAD)
+        rows[at, width : 2 * width] = (
+            feature_scale * inverse[at, width:] * (h - u * back)
+        ).astype(BF16)
+        high, low = split(kf * cs)
+        kc_high, kc_low = split(mm(high, pick6) + mm(low, pick6))
+        rows[at, 2 * width : 2 * width + 128] = kc_high
+        rows[at, 2 * width + 128 :] = kc_low
+
+    def key_step(i, carry):
+        key_pass(pl.multiple_of(i * chunk, 16), chunk)
+        return carry
+
+    lax.fori_loop(0, padded // chunk, key_step, 0)
+    key_pass(padded, tok_n)
+
+    hit = gene_lane == idx_col
+    tok_pred = pred_x[padded:, 0:1]
+    base_row = jnp.transpose(pred_x[0:padded, :])[0:1, :]
+    moved = jnp.sum(jnp.where(hit, tok_pred, 0.0), axis=0, keepdims=True)
+    final = jnp.where(keep_row > 0.5, base_row, moved)
+    pred_ref[...] = final[:, :gene_count]
+
+    share = width // dp_n
+    cols = grads.shape[2]
+    full = lax.dot_general(
+        normed[...], rows[...], (((0,), (0,)), ((), ())), preferred_element_type=F32
+    )
+    full = jnp.concatenate(
+        [full[:, : 2 * width], full[:, 2 * width : cols] + full[:, cols:]], axis=1
+    )
+    for j in range(dp_n):
+        grads[j] = full[j * share : (j + 1) * share, :]
+    core = lax.rem(dp, 2)
+    chip = dp // 2
+    chips = dp_n // 2
+    copies = []
+    for z in range(chips):
+        copies.append(
+            send(
+                grads.at[2 * z + 1 - core],
+                core_recv.at[z],
+                (core_s, core_r),
+                z,
+                z,
+                {"dp": 2 * chip + 1 - core},
+            )
+        )
+    for copy in copies:
+        copy.wait()
+    copies = []
+    for k in range(1, chips):
+        z = lax.rem(chip + k, chips)
+        z_send[k] = (grads[2 * z + core] + core_recv[z]).astype(BF16)
+        copies.append(
+            send(z_send.at[k], z_recv.at[k], (z_s, z_r), k, k, {"dp": 2 * z + core})
+        )
+    total = grads[2 * chip + core] + core_recv[chip]
+    for copy in copies:
+        copy.wait()
+    for k in range(1, chips):
+        total = total + z_recv[k].astype(F32)
+    span = ctx_recv.shape[2]
+    for s in range(ctx_n):
+        lo = 256 * min(s, 2)
+        part[s] = total[:, lo : lo + span]
+    copies = []
+    for k in range(1, ctx_n):
+        dest = lax.rem(ctx + k, ctx_n)
+        copies.append(
+            send(part.at[dest], ctx_recv.at[k], (last_s, last_r), k, k, {"ctx": dest})
+        )
+    for copy in copies:
+        copy.wait()
+    window = part[ctx]
+    for k in range(1, ctx_n):
+        window = window + ctx_recv[k]
+    tail_part = window[:, 256:]
+    head_of = lax.broadcasted_iota(jnp.int32, (1, width), 1) // HEAD
+    value_grad = jnp.zeros((share, width), F32)
+    for h in range(HEADS):
+        value_grad = value_grad + tail_part[:, h : h + 1] * jnp.where(head_of == h, w_row, 0.0)
+    result = window[:, 0:288]
+    result = jnp.where(ctx == 1, window[:, 32:320], result)
+    mixed = jnp.concatenate([window[:, 64:256], value_grad[:, 0:96]], axis=1)
+    result = jnp.where(ctx == 2, mixed, result)
+    result = jnp.where(ctx == 3, value_grad[:, 96:384], result)
+    grad_ref[...] = result
+
+
+def fused(
+    gene_ids,
+    counts,
+    values,
+    lengths,
+    bin_edges,
+    bin_table,
+    value_weight,
+    in_weight,
+    out_weight,
+    gene_table,
+    zero_embed,
+    qkv_weight,
+    proj_weight,
+    readout,
+    targets,
+):
+    ctx_n = lax.axis_size("ctx")
+    dp_n = lax.axis_size("dp")
+    gene_count, width = gene_table.shape
+    padded = -(-gene_count // 128) * 128
+    tok_n = gene_ids.shape[1]
+    chunk = padded // CHUNKS
+    total = padded + tok_n
+    share = width // dp_n
+    gene_table = jnp.pad(gene_table, ((0, padded - gene_count), (0, 0)))
+    targets = jnp.pad(targets, ((0, 0), (0, padded - gene_count)))
+    vmem = pl.BlockSpec(memory_space=pltpu.VMEM)
+    smem = pl.BlockSpec(memory_space=pltpu.SMEM)
+    dma = pltpu.SemaphoreType.DMA
+    cols = 2 * width + 128
+    return pl.pallas_call(
+        functools.partial(kernel, gene_count, chunk),
+        out_shape=(
+            jax.ShapeDtypeStruct((1, gene_count), F32),
+            jax.ShapeDtypeStruct((share, 3 * width // ctx_n), F32),
+        ),
+        in_specs=[vmem] * 3 + [smem] * 2 + [vmem] * 10,
+        out_specs=(vmem, vmem),
+        scratch_shapes=[
+            pltpu.VMEM((64, width), F32),
+            pltpu.VMEM((256, 256), BF16),
+            pltpu.VMEM((width, width), BF16),
+            pltpu.VMEM((width, width), BF16),
+            pltpu.VMEM((ctx_n, 8, tok_n), F32),
+            pltpu.VMEM((dp_n, 8, tok_n), F32),
+            pltpu.VMEM((dp_n, tok_n, width), BF16),
+            pltpu.VMEM((dp_n, tok_n, width), BF16),
+            pltpu.VMEM((total, width), BF16),
+            pltpu.VMEM((total, 2 * width), F32),
+            pltpu.VMEM((total, 2 * width), F32),
+            pltpu.VMEM((total, width), F32),
+            pltpu.VMEM((total, 2 * width + 256), BF16),
+            pltpu.VMEM((total, 128), F32),
+            pltpu.VMEM((total, 128), F32),
+            pltpu.VMEM((total, 128), F32),
+            pltpu.VMEM((total, 128), F32),
+            pltpu.VMEM((ctx_n, 8, width), F32),
+            pltpu.VMEM((ctx_n, 8, width), F32),
+            pltpu.VMEM((dp_n, share, cols), F32),
+            pltpu.VMEM((dp_n // 2, share, cols), F32),
+            pltpu.VMEM((dp_n // 2, share, cols), BF16),
+            pltpu.VMEM((dp_n // 2, share, cols), BF16),
+            pltpu.VMEM((ctx_n, share, 384), F32),
+            pltpu.VMEM((ctx_n, share, 384), F32),
+        ]
+        + [dma((n,)) for n in (ctx_n, dp_n, dp_n, ctx_n, ctx_n, dp_n // 2, dp_n // 2, ctx_n) for _ in range(2)],
+        compiler_params=pltpu.CompilerParams(
+            collective_id=0, has_side_effects=True, vmem_limit_bytes=60 * 2**20
+        ),
+        cost_estimate=pl.CostEstimate(
+            flops=20 * total * width * width, bytes_accessed=6 * 2**20, transcendentals=4 * total * width
+        ),
+    )(
+        gene_ids,
+        counts,
+        values,
+        lengths,
+        bin_edges,
+        bin_table,
+        value_weight[None, :],
+        in_weight,
+        out_weight,
+        gene_table,
+        zero_embed[None, :],
+        qkv_weight,
+        proj_weight,
+        readout[None, :],
+        targets,
+    )
+
+
+def program(*args):
+    ctx_n = lax.axis_size("ctx")
+    dp_n = lax.axis_size("dp")
+    width = args[9].shape[1]
+    fits = ctx_n == 4 and dp_n == 8 and width == 384 and args[0].shape[1] == 128
+    fits = fits and args[9].shape[0] <= 2432
+    return (fused if fits else body)(*args)
+
+
 def solution(mesh):
     return jax.shard_map(
-        body,
+        program,
         mesh=mesh,
         in_specs=(
             P("dp", "ctx"),

time: 327 us -> 86.7 us (0.27); the launches traced: 323 us -> 86.3 us
  waiting for transfers between devices: 137 us -> 0 us
  Pallas kernels: 0 us -> 74.2 us
  matrix products: 60.6 us -> 0 us
  local copies, waits for them, and re-layouts: 48.6 us -> 10.8 us
  other arithmetic: 33.6 us -> 0 us
  blocking collectives: 19.1 us -> 0 us
  between operations: 15.5 us -> 1.29 us
  starting transfers between devices: 8.65 us -> 0 us
    pallas_call x0 -> x1, Pallas kernels: none -> 74.2 us  [fused(): pl.pallas_call(functools.partial(kernel, gene_count, chunk), out_shape=(j...]
    dot_general x14 -> x0, matrix products: 60.6 us -> none  [the longest x1 7.85 us: summarize(): summary = jnp.einsum('ghj,ghe->hje', key_feat, value_raw, precision=highest)]
    psum x2 -> x0, waiting for transfers between devices: 44.1 us -> none  [the longest x1 24.2 us: body(): grad_summary, grad_total = lax.psum((part_gsummary, part_gtotal), 'ctx')]
    reduce_scatter x1 -> x0, waiting for transfers between devices: 35.1 us -> none  [body(): lax.psum_scatter(lax.dot_general(normed, grad_rows, (((0,), (0,)), ((), (...]
    all_gather x2 -> x0, waiting for transfers between devices: 29.9 us -> none  [the longest x1 25.9 us: encode(): lax.all_gather(out_weight, 'dp', axis=0, tiled=True)]
    unnamed x7 -> x0, waiting for transfers between devices: 24.7 us -> none
    reduce_sum x6 -> x0, other arithmetic: 22 us -> none  [the longest x1 8.95 us: summarize(): return (summary, jnp.sum(key_feat, axis=0))]
    psum x2 -> x0, blocking collectives: 19.1 us -> none  [the longest x1 9.96 us: body(): summary, key_total = lax.psum((part_summary, part_total), 'ctx')]
  transfers between devices with their start and end apart: 8 -> 0, of which waited for: 8 -> 0; matrix products, arithmetic and copies ran while one was open for 11% -> 0% of each run, Pallas kernels for 0% -> 0%
where the time goes in v1:
time: 86.7 us; the launch traced here: 86.3 us
  Pallas kernels  74.2 us (86%)
  local copies, waits for them, and re-layouts  10.8 us (12%)
  between operations  1.29 us (1%)
    pallas_call x1, Pallas kernels, fused(): pl.pallas_call(functools.partial(kernel, gene_count, chunk), out_shape=(j...  74.2 us
    pad x1, local copies, waits for them, and re-layouts, fused(): gene_table = jnp.pad(gene_table, ((0, padded - gene_count), (0, 0)))  2.96 us
    unnamed x2, local copies, waits for them, and re-layouts  2.82 us

profile of v1, /device:TPU:0, one launch (start us, length us, event | category | flops | bytes accessed | tf_op | source)
XLA Modules:
  0.0 86.3 jit_solution(13038428633050963454)
XLA Ops:
  1.3 1.2 %broadcast_in_dim.9.vweight_ref = f32[1,384]{1,0:T(1,128)} reshape(f32[384]{0:T(512)} %param.21) | data formatting | bytes 3072 | tf_op jit(solution)/shard_map/broadcast_in_dim | solution.py:730
  2.5 1.3 %broadcast_in_dim.10.zero_ref = bf16[1,384]{1,0:T(2,128)(2,1)} reshape(bf16[384]{0:T(512)(128)(2,1)} %param.25) | data formatting | bytes 1536 | tf_op jit(solution)/shard_map/broadcast_in_dim | solution.py:734
  3.8 1.2 %broadcast_in_dim.11.readout_ref = f32[1,384]{1,0:T(1,128)} reshape(f32[384]{0:T(512)} %param.28) | data formatting | bytes 3072 | tf_op jit(solution)/shard_map/broadcast_in_dim | solution.py:737
  5.0 1.3 %pad.9.targets_ref = f32[1,2432]{1,0:T(1,128)} pad(f32[1,2408]{1,0:T(1,128)} %param.29, f32[]{:T(128)} %constant.4.clone.1), padding=0_0x0_24 | pad | bytes 19364 | tf_op jit(solution)/shard_map/jit(_pad)/pad | solution.py:676
  6.3 3.0 %pad.8.gene_ref = bf16[2432,384]{1,0:T(8,128)(2,1)} pad(bf16[2408,384]{1,0:T(8,128)(2,1)} %param.24, bf16[]{:T(256)} %constant.3.clone.1), padding=0_24x0_0 | pad | bytes 3717122 | tf_op jit(solution)/shard_map/jit(_pad)/pad | solution.py:675
  9.3 74.2 %shard_map.158 = (f32[1,2408]{1,0:T(1,128)}, f32[48,288]{1,0:T(8,128)}) custom-call(s32[1,128]{1,0:T(1,128)} %ids_ref.1, s32[1,128]{1,0:T(1,128)} %counts_ref.1, f32[1,128]{1,0:T(1,128)} %values_ref.1, s32[1]{0:T(128)S(6)} %copy.19.lengths_ref, s32[1,50]{1,0:T(1,128)} %edges_ref.1, bf16[51,384]{1,0:T(8,128)(2,1)} %table_ref.1, ...), custom_call_target="tpu_custom_call" | custom-call | flops 7549747200 | bytes 6291456 | tf_op jit(solution)/shard_map/pallas_call | solution.py:681
  83.5 1.3 %copy.20 = f32[1,2408]{1,0:T(1,128)} copy(f32[1,2408]{1,0:T(1,128)} %get-tuple-element.4) | data formatting | bytes 19264
  84.8 1.5 %copy.21 = f32[48,288]{1,0:T(8,128)} copy(f32[48,288]{1,0:T(8,128)} %get-tuple-element.5) | data formatting | bytes 110592

commit v2 on v1

--- a/solution.py
+++ b/solution.py
@@ -236,15 +236,13 @@
     return high, (x - high.astype(F32)).astype(BF16)
 
 
-def head_sum(x, ones):
-    high, low = split(x)
+def head_sum(x, ones, exact=False):
+    pieces = split(x) if exact else (x.astype(BF16),)
     parts = []
     for start in range(0, x.shape[1], 256):
         width = min(256, x.shape[1] - start)
         block = ones[:width, :width]
-        parts.append(
-            mm(high[:, start : start + width], block) + mm(low[:, start : start + width], block)
-        )
+        parts.append(sum(mm(piece[:, start : start + width], block) for piece in pieces))
     return jnp.concatenate(parts, axis=1)
 
 
@@ -292,9 +290,12 @@
     table,
     ones,
     wvw_hi,
-    wvw_lo,
+    genes,
+    target_row,
     slots,
     tokens,
+    ff_pair,
+    ff_core,
     ff_send,
     ff_recv,
     normed,
@@ -308,26 +309,36 @@
     pred_x,
     sums1,
     sums2,
-    grads,
-    core_recv,
-    z_send,
-    z_recv,
+    grads_q,
+    core_q,
+    zs_q,
+    zr_q,
+    grads_k,
+    core_k,
+    zs_k,
+    zr_k,
     part,
     ctx_recv,
     slot_s,
     slot_r,
     tok_s,
     tok_r,
+    pair_s,
+    pair_r,
     ff_s,
     ff_r,
     one_s,
     one_r,
     two_s,
     two_r,
-    core_s,
-    core_r,
-    z_s,
-    z_r,
+    cq_s,
+    cq_r,
+    zq_s,
+    zq_r,
+    ck_s,
+    ck_r,
+    zk_s,
+    zk_r,
     last_s,
     last_r,
 ):
@@ -335,10 +346,16 @@
     dp = lax.axis_index("dp")
     ctx_n = slots.shape[0]
     dp_n = tokens.shape[0]
-    padded = gene_ref.shape[0]
+    padded = genes.shape[0]
     width = gene_ref.shape[1]
     tok_n = ids_ref.shape[1]
     cap = tok_n // ctx_n
+    core = lax.rem(dp, 2)
+    chip = dp // 2
+    chips = dp_n // 2
+    vweight = vweight_ref[...].reshape(1, width)
+    zero = zero_ref[...].astype(F32).reshape(1, width)
+    readout = readout_ref[...].reshape(1, width)
 
     barrier = pltpu.get_barrier_semaphore()
     for k in range(1, ctx_n):
@@ -378,17 +395,18 @@
     hrow = lax.broadcasted_iota(jnp.int32, (256, 256), 0) // HEAD
     hcol = lax.broadcasted_iota(jnp.int32, (256, 256), 1) // HEAD
     ones[...] = jnp.where(hrow == hcol, 1.0, 0.0).astype(BF16)
-    readout = readout_ref[...]
     w_col = jnp.sum(proj_ref[...].astype(F32) * readout, axis=1, keepdims=True)
     w_row = jnp.transpose(jnp.broadcast_to(w_col, (width, 128)))[0:1, :]
-    v_dot = head_sum(qkv_ref[:, 2 * width :].astype(F32) * w_row, ones)
-    v_high, v_low = split(v_dot)
-    wvw_hi[...] = v_high
-    wvw_lo[...] = v_low
+    v_dot = head_sum(qkv_ref[:, 2 * width :].astype(F32) * w_row, ones, True)
+    wvw_hi[...] = v_dot.astype(BF16)
     table[...] = jnp.zeros_like(table)
     table[0 : table_ref.shape[0], :] = table_ref[...].astype(F32)
     table_b = table[...].astype(BF16)
-    target_x[0:padded, :] = lanes_to_rows(targets_ref[...])
+    target_row[...] = jnp.zeros_like(target_row)
+    target_row[:, 0:gene_count] = targets_ref[...]
+    target_x[0:padded, :] = lanes_to_rows(target_row[...])
+    genes[0:gene_count, :] = gene_ref[...].astype(F32)
+    genes[gene_count:, :] = jnp.zeros((padded - gene_count, width), F32)
     for copy in copies:
         copy.wait()
 
@@ -430,9 +448,9 @@
 
     gene_lane = lax.broadcasted_iota(jnp.int32, (tok_n, padded), 1).astype(F32)
     hit = gene_lane == idx_col
-    token_base = mm(jnp.where(hit, 1.0, 0.0).astype(BF16), gene_ref[...])
+    token_base = mm(jnp.where(hit, 1.0, 0.0).astype(BF16), genes[...].astype(BF16))
     taken = jnp.sum(jnp.where(hit, 1.0, 0.0), axis=0, keepdims=True)
-    tok_target = jnp.sum(jnp.where(hit, targets_ref[...], 0.0), axis=1, keepdims=True)
+    tok_target = jnp.sum(jnp.where(hit, target_row[...], 0.0), axis=1, keepdims=True)
     in_range = lax.broadcasted_iota(jnp.int32, (1, padded), 1) < gene_count
     keep_row = jnp.where(in_range & (taken < 0.5), 1.0, 0.0)
     keep_x[0:padded, :] = lanes_to_rows(keep_row)
@@ -440,29 +458,48 @@
     keep_x[padded:, :] = jnp.broadcast_to(tok_live, (tok_n, 128))
     target_x[padded:, :] = jnp.broadcast_to(tok_target, (tok_n, 128))
 
-    pick = lax.broadcasted_iota(jnp.int32, (tok_n, table.shape[0]), 1).astype(F32)
+    pick = lax.broadcasted_iota(jnp.int32, (1, table.shape[0]), 1).astype(F32)
 
     def embed(bin_c, val_c):
         one_hot = jnp.where(bin_c == pick, 1.0, 0.0).astype(BF16)
-        return mm(one_hot, table_b) + val_c * vweight_ref[...]
+        return mm(one_hot, table_b) + val_c * vweight
 
     def feed(emb):
         pre = mm(rms(emb).astype(BF16), in_ref[...])
         act = (pre / (1.0 + jnp.exp(-pre))).astype(BF16)
         return mm(act, out_ref[...])
 
+    for copy in copies:
+        copy.wait()
+
+    def unpack(cells):
+        got = jnp.concatenate(
+            [jnp.transpose(jnp.concatenate([tokens[c]] * (128 // 8), axis=0)) for c in cells], axis=0
+        )
+        return embed(got[:, 0:1], got[:, 1:2])
+
+    half = feed(unpack([2 * z + 1 - core for z in range(chips)]))
+    pair_copies = []
+    for z in range(chips):
+        ff_pair[z] = half[z * tok_n : (z + 1) * tok_n].astype(BF16)
+        pair_copies.append(
+            send(
+                ff_pair.at[z], ff_core.at[z], (pair_s, pair_r), z, z, {"dp": 2 * chip + 1 - core}
+            )
+        )
+    turn = [lax.rem(chip + k, chips) for k in range(chips)]
+    own_emb = unpack([2 * z + core for z in turn])
+    half = feed(own_emb)
+    for copy in pair_copies:
+        copy.wait()
     ff_copies = []
-    for k in range(1, dp_n):
-        copies[k - 1].wait()
-    for k in range(1, dp_n):
-        other = lax.rem(dp + k, dp_n)
-        got = jnp.transpose(jnp.concatenate([tokens[other]] * (128 // 8), axis=0))
-        ff_send[k] = feed(embed(got[:, 0:1], got[:, 1:2])).astype(BF16)
+    for k in range(1, chips):
+        mixed = half[k * tok_n : (k + 1) * tok_n] + ff_core[turn[k]].astype(F32)
+        ff_send[k] = mixed.astype(BF16)
         ff_copies.append(
-            send(ff_send.at[k], ff_recv.at[k], (ff_s, ff_r), k, k, {"dp": other})
-        )
-    own_emb = embed(bin_col, val_col)
-    own_mix = own_emb + feed(own_emb)
+            send(ff_send.at[k], ff_recv.at[k], (ff_s, ff_r), k, k, {"dp": 2 * turn[k] + core})
+        )
+    own_mix = own_emb[0:tok_n] + half[0:tok_n] + ff_core[chip].astype(F32)
 
     def features(start, count, gene_input):
         at = pl.ds(start, count)
@@ -473,11 +510,11 @@
             jnp.sum(gi * readout, axis=1, keepdims=True), (count, 128)
         )
         raw = mm(nb, qkv_ref[:, : 2 * width])
-        inv = lax.rsqrt(head_sum(raw * raw, ones) * (1.0 / HEAD) + norm_eps)
+        inv = lax.rsqrt(head_sum(raw * raw, ones, True) * (1.0 / HEAD) + norm_eps)
         u = raw * inv
         unit[at, :] = u
         inverse[at, :] = inv
-        vw = mm(nb, wvw_hi[...]) + mm(nb, wvw_lo[...])
+        vw = mm(nb, wvw_hi[...])
         vwx[at, :] = vw
         kf = jnp.exp(feature_scale * u[:, width:]) * keep_x[at, 0:1]
         return (
@@ -485,23 +522,22 @@
             jnp.sum(kf * vw, axis=0, keepdims=True),
         )
 
-    zero = zero_ref[...].astype(F32)
     none = jnp.zeros((1, width), F32)
 
     def first_pass(i, carry):
         start = pl.multiple_of(i * chunk, 16)
-        a, b = features(start, chunk, gene_ref[pl.ds(start, chunk), :].astype(F32) + zero)
+        a, b = features(start, chunk, genes[pl.ds(start, chunk), :] + zero)
         return carry[0] + a, carry[1] + b
 
     kt, us = lax.fori_loop(0, padded // chunk, first_pass, (none, none))
     for copy in ff_copies:
         copy.wait()
-    for k in range(1, dp_n):
+    for k in range(1, chips):
         own_mix = own_mix + ff_recv[k].astype(F32)
     a, b = features(padded, tok_n, token_base + own_mix.astype(BF16).astype(F32))
     kt, us = kt + a, us + b
 
-    def over_ctx(buffer, sems, x, y):
+    def ctx_start(buffer, sems, x, y):
         row_at = lax.broadcasted_iota(jnp.int32, (8, width), 0)
         buffer[ctx] = jnp.where(row_at == 0, x, jnp.where(row_at == 1, y, 0.0))
         sent = []
@@ -509,6 +545,9 @@
             sent.append(
                 send(buffer.at[ctx], buffer.at[ctx], sems, k, k, {"ctx": lax.rem(ctx + k, ctx_n)})
             )
+        return sent
+
+    def ctx_finish(buffer, sent):
         for copy in sent:
             copy.wait()
         total = buffer[0]
@@ -516,7 +555,7 @@
             total = total + buffer[s]
         return total[0:1], total[1:2]
 
-    kt, us = over_ctx(sums1, (one_s, one_r), kt, us)
+    kt, us = ctx_finish(sums1, ctx_start(sums1, (one_s, one_r), kt, us))
     scale = 1.0 / math.sqrt(gene_count * ctx_n * dp_n)
 
     def query_pass(start, count, carry):
@@ -544,7 +583,44 @@
         (none, none),
     )
     cs, ts = query_pass(padded, tok_n, (cs, ts))
-    cs, ts = over_ctx(sums2, (two_s, two_r), cs, ts)
+    sent = ctx_start(sums2, (two_s, two_r), cs, ts)
+
+    share = width // dp_n
+
+    def core_start(part_grad, grads, recv, sems):
+        for j in range(dp_n):
+            grads[j] = part_grad[j * share : (j + 1) * share, :]
+        return [
+            send(
+                grads.at[2 * z + 1 - core], recv.at[z], sems, z, z, {"dp": 2 * chip + 1 - core}
+            )
+            for z in range(chips)
+        ]
+
+    def z_start(core_copies, grads, recv, out, into, sems):
+        for copy in core_copies:
+            copy.wait()
+        started = []
+        for k in range(1, chips):
+            z = lax.rem(chip + k, chips)
+            out[k] = (grads[2 * z + core] + recv[z]).astype(BF16)
+            started.append(send(out.at[k], into.at[k], sems, k, k, {"dp": 2 * z + core}))
+        return grads[2 * chip + core] + recv[chip], started
+
+    def z_finish(total, started, into):
+        for copy in started:
+            copy.wait()
+        for k in range(1, chips):
+            total = total + into[k].astype(F32)
+        return total
+
+    def outer(lo, hi):
+        return lax.dot_general(
+            normed[...], rows[:, lo:hi], (((0,), (0,)), ((), ())), preferred_element_type=F32
+        )
+
+    copies_q = core_start(outer(0, width), grads_q, core_q, (cq_s, cq_r))
+    cs, ts = ctx_finish(sums2, sent)
     pick6 = jnp.where(
         lax.broadcasted_iota(jnp.int32, (width, 128), 0) // HEAD
         == lax.broadcasted_iota(jnp.int32, (width, 128), 1),
@@ -561,17 +637,19 @@
         rows[at, width : 2 * width] = (
             feature_scale * inverse[at, width:] * (h - u * back)
         ).astype(BF16)
-        high, low = split(kf * cs)
-        kc_high, kc_low = split(mm(high, pick6) + mm(low, pick6))
-        rows[at, 2 * width : 2 * width + 128] = kc_high
-        rows[at, 2 * width + 128 :] = kc_low
+        rows[at, 2 * width :] = mm((kf * cs).astype(BF16), pick6).astype(BF16)
 
     def key_step(i, carry):
         key_pass(pl.multiple_of(i * chunk, 16), chunk)
         return carry
 
-    lax.fori_loop(0, padded // chunk, key_step, 0)
+    steps = padded // chunk
+    lax.fori_loop(0, steps // 2, key_step, 0)
+    total_q, started_q = z_start(copies_q, grads_q, core_q, zs_q, zr_q, (zq_s, zq_r))
+    lax.fori_loop(steps // 2, steps, key_step, 0)
     key_pass(padded, tok_n)
+    copies_k = core_start(outer(width, 2 * width + 128), grads_k, core_k, (ck_s, ck_r))
+    total_k, started_k = z_start(copies_k, grads_k, core_k, zs_k, zr_k, (zk_s, zk_r))
 
     hit = gene_lane == idx_col
     tok_pred = pred_x[padded:, 0:1]
@@ -580,45 +658,9 @@
     final = jnp.where(keep_row > 0.5, base_row, moved)
     pred_ref[...] = final[:, :gene_count]
 
-    share = width // dp_n
-    cols = grads.shape[2]
-    full = lax.dot_general(
-        normed[...], rows[...], (((0,), (0,)), ((), ())), preferred_element_type=F32
-    )
-    full = jnp.concatenate(
-        [full[:, : 2 * width], full[:, 2 * width : cols] + full[:, cols:]], axis=1
-    )
-    for j in range(dp_n):
-        grads[j] = full[j * share : (j + 1) * share, :]
-    core = lax.rem(dp, 2)
-    chip = dp // 2
-    chips = dp_n // 2
-    copies = []
-    for z in range(chips):
-        copies.append(
-            send(
-                grads.at[2 * z + 1 - core],
-                core_recv.at[z],
-                (core_s, core_r),
-                z,
-                z,
-                {"dp": 2 * chip + 1 - core},
-            )
-        )
-    for copy in copies:
-        copy.wait()
-    copies = []
-    for k in range(1, chips):
-        z = lax.rem(chip + k, chips)
-        z_send[k] = (grads[2 * z + core] + core_recv[z]).astype(BF16)
-        copies.append(
-            send(z_send.at[k], z_recv.at[k], (z_s, z_r), k, k, {"dp": 2 * z + core})
-        )
-    total = grads[2 * chip + core] + core_recv[chip]
-    for copy in copies:
-        copy.wait()
-    for k in range(1, chips):
-        total = total + z_recv[k].astype(F32)
+    total = jnp.concatenate(
+        [z_finish(total_q, started_q, zr_q), z_finish(total_k, started_k, zr_k)], axis=1
+    )
     span = ctx_recv.shape[2]
     for s in range(ctx_n):
         lo = 256 * min(s, 2)
@@ -672,12 +714,10 @@
     chunk = padded // CHUNKS
     total = padded + tok_n
     share = width // dp_n
-    gene_table = jnp.pad(gene_table, ((0, padded - gene_count), (0, 0)))
-    targets = jnp.pad(targets, ((0, 0), (0, padded - gene_count)))
     vmem = pl.BlockSpec(memory_space=pltpu.VMEM)
     smem = pl.BlockSpec(memory_space=pltpu.SMEM)
     dma = pltpu.SemaphoreType.DMA
-    cols = 2 * width + 128
+    chips = dp_n // 2
     return pl.pallas_call(
         functools.partial(kernel, gene_count, chunk),
         out_shape=(
@@ -690,30 +730,37 @@
             pltpu.VMEM((64, width), F32),
             pltpu.VMEM((256, 256), BF16),
             pltpu.VMEM((width, width), BF16),
-            pltpu.VMEM((width, width), BF16),
+            pltpu.VMEM((padded, width), F32),
+            pltpu.VMEM((1, padded), F32),
             pltpu.VMEM((ctx_n, 8, tok_n), F32),
             pltpu.VMEM((dp_n, 8, tok_n), F32),
-            pltpu.VMEM((dp_n, tok_n, width), BF16),
-            pltpu.VMEM((dp_n, tok_n, width), BF16),
+            pltpu.VMEM((chips, tok_n, width), BF16),
+            pltpu.VMEM((chips, tok_n, width), BF16),
+            pltpu.VMEM((chips, tok_n, width), BF16),
+            pltpu.VMEM((chips, tok_n, width), BF16),
             pltpu.VMEM((total, width), BF16),
             pltpu.VMEM((total, 2 * width), F32),
             pltpu.VMEM((total, 2 * width), F32),
             pltpu.VMEM((total, width), F32),
-            pltpu.VMEM((total, 2 * width + 256), BF16),
+            pltpu.VMEM((total, 2 * width + 128), BF16),
             pltpu.VMEM((total, 128), F32),
             pltpu.VMEM((total, 128), F32),
             pltpu.VMEM((total, 128), F32),
             pltpu.VMEM((total, 128), F32),
             pltpu.VMEM((ctx_n, 8, width), F32),
             pltpu.VMEM((ctx_n, 8, width), F32),
-            pltpu.VMEM((dp_n, share, cols), F32),
-            pltpu.VMEM((dp_n // 2, share, cols), F32),
-            pltpu.VMEM((dp_n // 2, share, cols), BF16),
-            pltpu.VMEM((dp_n // 2, share, cols), BF16),
+            pltpu.VMEM((dp_n, share, width), F32),
+            pltpu.VMEM((chips, share, width), F32),
+            pltpu.VMEM((chips, share, width), BF16),
+            pltpu.VMEM((chips, share, width), BF16),
+            pltpu.VMEM((dp_n, share, width + 128), F32),
+            pltpu.VMEM((chips, share, width + 128), F32),
+            pltpu.VMEM((chips, share, width + 128), BF16),
+            pltpu.VMEM((chips, share, width + 128), BF16),
             pltpu.VMEM((ctx_n, share, 384), F32),
             pltpu.VMEM((ctx_n, share, 384), F32),
         ]
-        + [dma((n,)) for n in (ctx_n, dp_n, dp_n, ctx_n, ctx_n, dp_n // 2, dp_n // 2, ctx_n) for _ in range(2)],
+        + [dma((n,)) for n in (ctx_n, dp_n, chips, chips, ctx_n, ctx_n, chips, chips, chips, chips, ctx_n) for _ in range(2)],
         compiler_params=pltpu.CompilerParams(
             collective_id=0, has_side_effects=True, vmem_limit_bytes=60 * 2**20
         ),
@@ -727,14 +774,14 @@
         lengths,
         bin_edges,
         bin_table,
-        value_weight[None, :],
+        value_weight,
         in_weight,
         out_weight,
         gene_table,
-        zero_embed[None, :],
+        zero_embed,
         qkv_weight,
         proj_weight,
-        readout[None, :],
+        readout,
         targets,
     )
 

time: 86.7 us -> 64.1 us (0.74)
  Pallas kernels: 74.2 us -> 59.7 us
  local copies, waits for them, and re-layouts: 10.8 us -> 2.82 us
    pallas_call x1, Pallas kernels: 74.2 us -> 59.7 us  [fused(): pl.pallas_call(functools.partial(kernel, gene_count, chunk), out_shape=(j...]
    pad x2 -> x0, local copies, waits for them, and re-layouts: 4.26 us -> none  [the longest x1 2.96 us: fused(): gene_table = jnp.pad(gene_table, ((0, padded - gene_count), (0, 0)))]
    broadcast_in_dim x3 -> x0, local copies, waits for them, and re-layouts: 3.73 us -> none  [the longest x1 1.25 us: fused(): zero_embed[None, :]]
where the time goes in v2:
time: 64.1 us; the launch traced here: 63.8 us
  Pallas kernels  59.7 us (93%)
  local copies, waits for them, and re-layouts  2.82 us (4%)
  between operations  1.29 us (2%)
    pallas_call x1, Pallas kernels, fused(): pl.pallas_call(functools.partial(kernel, gene_count, chunk), out_shape=(j...  59.7 us
    unnamed x2, local copies, waits for them, and re-layouts  2.82 us

profile of v2, /device:TPU:0, one launch (start us, length us, event | category | flops | bytes accessed | tf_op | source)
XLA Modules:
  0.0 63.8 jit_solution(13809695284683604278)
XLA Ops:
  1.3 59.7 %shard_map.158 = (f32[1,2408]{1,0:T(1,128)}, f32[48,288]{1,0:T(8,128)}) custom-call(s32[1,128]{1,0:T(1,128)} %ids_ref.1, s32[1,128]{1,0:T(1,128)} %counts_ref.1, f32[1,128]{1,0:T(1,128)} %values_ref.1, s32[1]{0:T(128)S(6)} %copy.19.lengths_ref, s32[1,50]{1,0:T(1,128)} %edges_ref.1, bf16[51,384]{1,0:T(8,128)(2,1)} %table_ref.1, f32[384]{0:T(512)} %vweight_ref.1, ...), custom_call_target="tpu_custom_call" | custom-call | flops 7549747200 | bytes 6291456 | tf_op jit(solution)/shard_map/pallas_call | solution.py:721
  61.0 1.3 %copy.20 = f32[1,2408]{1,0:T(1,128)} copy(f32[1,2408]{1,0:T(1,128)} %get-tuple-element.4) | data formatting | bytes 19264
  62.3 1.5 %copy.21 = f32[48,288]{1,0:T(8,128)} copy(f32[48,288]{1,0:T(8,128)} %get-tuple-element.5) | data formatting | bytes 110592

commit v3 on v2

--- a/solution.py
+++ b/solution.py
@@ -290,6 +290,7 @@
     table,
     ones,
     wvw_hi,
+    wvw_lo,
     genes,
     target_row,
     slots,
@@ -398,7 +399,7 @@
     w_col = jnp.sum(proj_ref[...].astype(F32) * readout, axis=1, keepdims=True)
     w_row = jnp.transpose(jnp.broadcast_to(w_col, (width, 128)))[0:1, :]
     v_dot = head_sum(qkv_ref[:, 2 * width :].astype(F32) * w_row, ones, True)
-    wvw_hi[...] = v_dot.astype(BF16)
+    wvw_hi[...], wvw_lo[...] = split(v_dot)
     table[...] = jnp.zeros_like(table)
     table[0 : table_ref.shape[0], :] = table_ref[...].astype(F32)
     table_b = table[...].astype(BF16)
@@ -514,7 +515,7 @@
         u = raw * inv
         unit[at, :] = u
         inverse[at, :] = inv
-        vw = mm(nb, wvw_hi[...])
+        vw = mm(nb, wvw_hi[...]) + mm(nb, wvw_lo[...])
         vwx[at, :] = vw
         kf = jnp.exp(feature_scale * u[:, width:]) * keep_x[at, 0:1]
         return (
@@ -563,7 +564,7 @@
         u = unit[at, :width]
         qf = jnp.exp(feature_scale * u)
         den = head_sum(qf * kt, ones)
-        att = head_sum(qf * us, ones) / den
+        att = head_sum(qf * us, ones, True) / den
         predicted = base_dot[at, 0:1] + jnp.sum(att, axis=1, keepdims=True) * (1.0 / HEAD)
         pred_x[at, :] = jnp.broadcast_to(predicted, (count, 128))
         res = (predicted - target_x[at, 0:1]) * (scale * keep_x[at, 0:1])
@@ -637,7 +638,7 @@
         rows[at, width : 2 * width] = (
             feature_scale * inverse[at, width:] * (h - u * back)
         ).astype(BF16)
-        rows[at, 2 * width :] = mm((kf * cs).astype(BF16), pick6).astype(BF16)
+        rows[at, 2 * width :] = sum(mm(x, pick6) for x in split(kf * cs)).astype(BF16)
 
     def key_step(i, carry):
         key_pass(pl.multiple_of(i * chunk, 16), chunk)
@@ -729,6 +730,7 @@
         scratch_shapes=[
             pltpu.VMEM((64, width), F32),
             pltpu.VMEM((256, 256), BF16),
+            pltpu.VMEM((width, width), BF16),
             pltpu.VMEM((width, width), BF16),
             pltpu.VMEM((padded, width), F32),
             pltpu.VMEM((1, padded), F32),

time: 64.1 us -> 66 us (1.030)
  Pallas kernels: 59.7 us -> 61.6 us
    pallas_call x1, Pallas kernels: 59.7 us -> 61.6 us  [fused(): pl.pallas_call(functools.partial(kernel, gene_count, chunk), out_shape=(j...]
where the time goes in v3:
time: 66 us; the launch traced here: 65.7 us
  Pallas kernels  61.6 us (93%)
  local copies, waits for them, and re-layouts  2.82 us (4%)
  between operations  1.29 us (2%)
    pallas_call x1, Pallas kernels, fused(): pl.pallas_call(functools.partial(kernel, gene_count, chunk), out_shape=(j...  61.6 us
    unnamed x2, local copies, waits for them, and re-layouts  2.82 us

profile of v3, /device:TPU:0, one launch (start us, length us, event | category | flops | bytes accessed | tf_op | source)
XLA Modules:
  0.0 65.7 jit_solution(14418272968342709182)
XLA Ops:
  1.3 61.6 %shard_map.158 = (f32[1,2408]{1,0:T(1,128)}, f32[48,288]{1,0:T(8,128)}) custom-call(s32[1,128]{1,0:T(1,128)} %ids_ref.1, s32[1,128]{1,0:T(1,128)} %counts_ref.1, f32[1,128]{1,0:T(1,128)} %values_ref.1, s32[1]{0:T(128)S(6)} %copy.19.lengths_ref, s32[1,50]{1,0:T(1,128)} %edges_ref.1, bf16[51,384]{1,0:T(8,128)(2,1)} %table_ref.1, f32[384]{0:T(512)} %vweight_ref.1, ...), custom_call_target="tpu_custom_call" | custom-call | flops 7549747200 | bytes 6291456 | tf_op jit(solution)/shard_map/pallas_call | solution.py:722
  62.9 1.3 %copy.20 = f32[1,2408]{1,0:T(1,128)} copy(f32[1,2408]{1,0:T(1,128)} %get-tuple-element.4) | data formatting | bytes 19264
  64.2 1.5 %copy.21 = f32[48,288]{1,0:T(8,128)} copy(f32[48,288]{1,0:T(8,128)} %get-tuple-element.5) | data formatting | bytes 110592
